TPU v7x, 128 devices: a whole 4x4x4 slice. The times are simulated.
128 devices in a mesh: kr: 8 (over z, core), kc: 16 (over y, x).
Axes of the slice: x: 4, y: 4, z: 4, core: 2. Of those that a mesh axis runs over, the one named last changes fastest.
Arguments:
- trial: bfloat16 [256, 512], P(('kr', 'kc')), may hold values from -6 to 6
- screened: bfloat16 [16, 2048, 2048], P(None, None, 'kc'), may hold values from -0.125 to 0.125
- density: bfloat16 [4096, 2048, 128], P(('kr', 'kc')), may hold values from -0.15625 to 0.15625
- pair_rows: int32 [4096], P(('kr', 'kc')), may hold values from 0 to 31
- pair_cols: int32 [4096], P(('kr', 'kc')), may hold values from 0 to 15
- slot_momentum: int32 [256], P(('kr', 'kc')), may hold values from 0 to 15
- slot_count: int32 [256], P(('kr', 'kc')), may hold values from 1 to 16, as said below
Outputs:
- response: float32 [256, 512], P(('kr', 'kc'))
Inputs may be any that keep to these rules, and one draw needn't show every extreme that they name: `slot_count`: the first transfer slot always holds 16 listed pairs.
All inputs are finite; a program needn't handle non-finite values.
Results may differ from a plain program's by a relative error of at most 0.0029.
Values may be sent and summed in bfloat16 or wider, within the bound.
A program may use at most 192 MiB of HBM per device.

v0:
```python
import jax
import jax.numpy as jnp
from jax import lax
from jax.sharding import PartitionSpec as P

NCON = 8
NVAL = 8


def body(trial, screened, density, pair_rows, pair_cols, slot_momentum, slot_count):
    rows_kc = lax.axis_size("kc")
    row_width = trial.shape[1]
    high = lax.Precision.HIGHEST
    row_vectors = lax.all_gather(trial, "kc", axis=0, tiled=True)
    col_vectors = lax.all_gather(trial, "kr", axis=0, tiled=True)
    planes = screened.shape[1]
    col_block = screened.shape[2]
    slot_number = slot_momentum.shape[0]
    wanted = lax.all_gather(slot_momentum, "kc", axis=0, tiled=True)
    outgoing = jnp.take(screened, wanted, axis=0).reshape(rows_kc, slot_number, planes, col_block)
    weights = lax.all_to_all(outgoing, "kc", split_axis=0, concat_axis=3, tiled=True)[0]
    per_slot = density.shape[0] // slot_number
    cond_width = NCON * NCON
    densities = density.reshape(slot_number, per_slot, planes, density.shape[2])
    conduction = densities[..., :cond_width]
    valence = densities[..., cond_width:]
    screened_val = jnp.einsum(
        "sgh,sphw->spwg", weights, valence, preferred_element_type=jnp.float32
    ).astype(jnp.bfloat16)
    direct_kernel = jnp.einsum(
        "spgi,spwg->spiw", conduction, screened_val, preferred_element_type=jnp.float32
    )
    live_mask = jnp.arange(per_slot, dtype=jnp.int32)[None, :] < slot_count[:, None]
    direct_kernel = jnp.where(live_mask[:, :, None, None], direct_kernel, jnp.float32(0.0))
    pair_total = slot_number * per_slot
    direct_kernel = direct_kernel.reshape(pair_total, NCON, NCON, NVAL, NVAL)
    vec_count = row_width // (NCON * NVAL)
    row_pick = (
        pair_rows[:, None] == jnp.arange(row_vectors.shape[0], dtype=jnp.int32)[None, :]
    ).astype(jnp.bfloat16)
    col_pick = (
        pair_cols[:, None] == jnp.arange(col_vectors.shape[0], dtype=jnp.int32)[None, :]
    ).astype(jnp.bfloat16)
    trial_row = jnp.dot(row_pick, row_vectors, preferred_element_type=jnp.float32).reshape(
        pair_total, NCON, NVAL, vec_count
    )
    vec_col = jnp.dot(col_pick, col_vectors, preferred_element_type=jnp.float32).reshape(
        pair_total, NCON, NVAL, vec_count
    )
    y_row = jnp.einsum("pcdvw,pdwn->pcvn", direct_kernel, vec_col, precision=high).reshape(
        pair_total, row_width
    )
    y_col = jnp.einsum("pcdvw,pcvn->pdwn", direct_kernel, trial_row, precision=high).reshape(
        pair_total, row_width
    )
    row_part = jnp.dot(row_pick.astype(jnp.float32).T, y_row, precision=high)
    column_portion = jnp.dot(col_pick.astype(jnp.float32).T, y_col, precision=high)
    row_sum = lax.psum_scatter(row_part, "kc", scatter_dimension=0, tiled=True)
    col_sum = lax.psum_scatter(column_portion, "kr", scatter_dimension=0, tiled=True)
    return row_sum + col_sum


def solution(mesh):
    return jax.shard_map(
        body,
        mesh=mesh,
        in_specs=(
            P(("kr", "kc"), None),
            P(None, None, "kc"),
            P(("kr", "kc"), None, None),
            P(("kr", "kc")),
            P(("kr", "kc")),
            P(("kr", "kc")),
            P(("kr", "kc")),
        ),
        out_specs=P(("kr", "kc"), None),
        check_vma=False,
    )
```

profile of v0, /device:TPU:0, one launch (start us, length us, event | category | flops | bytes accessed | tf_op | source)
XLA Modules:
  0.0 513.6 jit_solution(2179818251182217391)
XLA Ops:
  6.5 1.3 fusion.26
  8.5 0.9 dynamic-update-slice
  9.4 16.6 %all-reduce = s32[32]{0:T(128)S(1)} all-reduce(s32[32]{0:T(128)S(1)} %dynamic-update-slice), channel_id=1, replica_groups=mesh['kr'=8,'kc'=16] {'kc'}, use_global_device_ids=true, to_apply=%add | all-reduce | flops 32 | bytes 256
  26.0 0.1 broadcast_in_dim.34
  26.1 10.7 %gather_fusion = bf16[32,2048,128]{2,1,0:T(8,128)(2,1)} fusion(bf16[16,2048,128]{2,1,0:T(8,128)(2,1)} %param.8, s32[1024]{0:T(1024)S(1)} %pad_clamp_fusion), kind=kCustom, calls=%fused_computation | custom fusion | bytes 33554560 | tf_op jit(solution)/shard_map/jit(_take)/gather | solution.py:20
  36.8 14.2 %broadcast_select_fusion = bf16[16,2,2048,128]{3,2,1,0:T(8,128)(2,1)} fusion(bf16[16,2,2048,128]{3,2,1,0:T(8,128)(2,1)} %bitcast.51, pred[16,2]{1,0:T(8,128)(4,1)S(1)} %broadcast_in_dim.34), kind=kLoop, calls=%fused_computation.1 | loop fusion | flops 8388608 | bytes 33554464 | tf_op jit(solution)/shard_map/jit(_take)/select_n | solution.py:20
  50.9 5.1 %all-to-all-start = ((bf16[16,2,2048,128]{3,2,1,0:T(8,128)(2,1)}), bf16[16,2,2048,128]{3,2,1,0:T(8,128)(2,1)}, u32[]{:S(2)}, u32[]{:S(2)}) async-start(bf16[16,2,2048,128]{3,2,1,0:T(8,128)(2,1)} %broadcast_select_fusion), calls=%async_computation | async-start | bytes 33554432 | tf_op jit(solution)/shard_map/all_to_all | solution.py:21
  56.1 22.6 %copy.35 = bf16[32,2048,128]{1,2,0:T(8,128)(2,1)} copy(bf16[32,2048,128]{2,1,0:T(8,128)(2,1)} %param.9) | data formatting | bytes 33554432 | tf_op args[2]
  78.7 8.3 %slice.10 = bf16[2,16,2048,64]{2,3,1,0:T(8,128)(2,1)} slice(bf16[2,16,2048,128]{2,3,1,0:T(8,128)(2,1)} %bitcast.49), slice={[0:2], [0:16], [0:2048], [64:128]} | slice | bytes 16777216 | tf_op jit(solution)/shard_map/slice | solution.py:26
  87.1 224.3 %all-gather.1 = bf16[16,2,512]{2,1,0:T(2,128)(2,1)S(1)} all-gather(bf16[1,2,512]{2,1,0:T(2,128)(2,1)S(1)} %bitcast.59), channel_id=1, replica_groups=mesh['kr'=8,'kc'=16] {'kc'}, dimensions={0}, use_global_device_ids=true | all-gather | bytes 34816 | tf_op jit(solution)/shard_map/all_gather | solution.py:14
  311.4 0.2 fusion.16
  311.6 1.8 copy.51
  313.4 13.0 %all-gather = bf16[8,2,512]{2,1,0:T(2,128)(2,1)S(1)} all-gather(bf16[1,2,512]{2,1,0:T(2,128)(2,1)S(1)} %bitcast.60), channel_id=1, replica_groups=mesh['kr'=8,'kc'=16] {'kr'}, dimensions={0}, use_global_device_ids=true | all-gather | bytes 18432 | tf_op jit(solution)/shard_map/all_gather | solution.py:15
  326.4 0.2 fusion.15
  326.7 1.7 copy.48
  328.4 0.6 dynamic-slice.3
  330.4 22.4 %copy.34 = bf16[1,2,2048,16,128]{2,4,3,1,0:T(8,128)(2,1)} copy(bf16[1,2,2048,16,128]{4,2,1,3,0:T(8,128)(2,1)} %bitcast.3) | data formatting | bytes 33554432 | tf_op jit(solution)/shard_map/all_to_all | solution.py:21
  352.8 21.5 %fusion.27 = f32[2,2048,1024]{1,2,0:S(1)} fusion(bf16[2,2048,1024]{1,2,0:T(8,128)(2,1)} %bitcast.54, bf16[2,2048,2048]{1,2,0:T(8,128)(2,1)} %bitcast.53), kind=kOutput, calls=%fused_computation.28 | convolution fusion | flops 17179869184 | bytes 41943040
  374.3 5.0 fusion.9
  379.4 4.8 copy.37
  384.1 4.4 reshape.52
  388.5 7.7 %copy.43 = f32[32,8,8,8,8]{3,4,1,2,0:T(8,128)} copy(f32[32,8,8,8,8]{0,4,3,2,1:T(8,128)S(1)} %reshape.52) | data formatting | bytes 1048576 | tf_op jit(solution)/shard_map/reshape | solution.py:36
  396.2 7.2 %copy.39 = f32[32,8,8,8,8]{4,3,2,1,0:T(8,128)} copy(f32[32,8,8,8,8]{0,4,3,2,1:T(8,128)S(1)} %reshape.52) | data formatting | bytes 1048576 | tf_op jit(solution)/shard_map/reshape | solution.py:36
  403.4 9.2 %convolution_bitcast_fusion = f32[32,8,8,8]{3,2,1,0:T(8,128)S(1)} fusion(f32[32,8,8,8,8]{3,4,1,2,0:T(8,128)} %copy.43, f32[32,8,8,8,1]{3,2,1,4,0:T(8,128)S(1)} %copy-done), kind=kOutput, calls=%fused_computation.6 | convolution fusion | flops 12582912 | bytes 655360 | tf_op jit(solution)/shard_map/pcdvw,pcvn->pdwn/dot_general | solution.py:53
  412.6 0.6 copy.45
  413.2 11.4 %convolution_bitcast_fusion.1 = f32[32,8,8,8]{3,2,1,0:T(8,128)S(1)} fusion(f32[32,8,8,8,8]{4,3,2,1,0:T(8,128)} %copy.39, f32[32,8,8,8,1]{3,2,1,4,0:T(8,128)} %copy.48), kind=kOutput, calls=%fused_computation.7 | convolution fusion | flops 12582912 | bytes 655360 | tf_op jit(solution)/shard_map/pcdvw,pdwn->pcvn/dot_general | solution.py:50
  424.5 0.6 copy.41
  425.1 1.0 fusion.18
  426.1 0.3 fusion.20
  426.4 25.5 %all-reduce.2 = f32[16,512]{1,0:T(8,128)S(1)} all-reduce(f32[16,512]{1,0:T(8,128)S(1)} %fusion.20), channel_id=3, replica_groups=mesh['kr'=8,'kc'=16] {'kr'}, use_global_device_ids=true, to_apply=%region_1.2.clone | all-reduce | flops 8192 | bytes 65536
  451.9 53.5 %all-reduce.5.cloned.1.call-done = f32[32,512]{1,0:T(8,128)} async-done(((f32[32,512]{1,0:T(8,128)}), f32[32,512]{1,0:T(8,128)}) %all-reduce.5.cloned.1.call-update) | async-done | bytes 65552
  505.4 1.3 dynamic-slice_add_fusion
  (22 shorter events, 0.2 us)
Async XLA Ops:
  50.9 279.5 %all-to-all-start = ((bf16[16,2,2048,128]{3,2,1,0:T(8,128)(2,1)}), bf16[16,2,2048,128]{3,2,1,0:T(8,128)(2,1)}, u32[]{:S(2)}, u32[]{:S(2)}) async-start(bf16[16,2,2048,128]{3,2,1,0:T(8,128)(2,1)} %broadcast_select_fusion), calls=%async_computation | async-start | bytes 33554432 | tf_op jit(solution)/shard_map/all_to_all | solution.py:21
  56.1 449.3 %all-reduce.5.cloned.1.call-start = ((), (), s32[]{:S(2)}) async-start(), calls=%async_computation.1 | async-start | bytes 131072
  78.7 8.3 %copy-start.1 = (bf16[2,512]{1,0:T(2,128)(2,1)S(1)}, bf16[2,512]{1,0:T(2,128)(2,1)}, u32[]{:S(2)}) copy-start(bf16[2,512]{1,0:T(2,128)(2,1)} %param.7) | copy-start | bytes 6148
  78.7 232.6 %copy-start.2 = (s32[32]{0:T(128)S(1)}, s32[32]{0:T(128)}, u32[]{:S(2)}) copy-start(s32[32]{0:T(128)} %param.10) | copy-start | bytes 388
  78.7 247.7 %copy-start.3 = (s32[32]{0:T(128)S(1)}, s32[32]{0:T(128)}, u32[]{:S(2)}) copy-start(s32[32]{0:T(128)} %param.11) | copy-start | bytes 388
  78.7 249.7 %copy-start.5 = (u32[128]{0:T(128)S(1)}, u32[128]{0:T(128)}, u32[]{:S(2)}) copy-start(u32[128]{0:T(128)} %constant.36) | copy-start | bytes 1540
  78.7 251.6 %copy-start.4 = (s32[2]{0:T(128)S(1)}, s32[2]{0:T(128)}, u32[]{:S(2)}) copy-start(s32[2]{0:T(128)} %param.13) | copy-start | bytes 28
  384.1 19.3 %copy-start = (f32[32,8,8,8,1]{3,2,1,4,0:T(8,128)S(1)}, f32[32,8,8,8,1]{3,2,1,4,0:T(8,128)}, u32[]{:S(2)}) copy-start(f32[32,8,8,8,1]{3,2,1,4,0:T(8,128)} %copy.51) | copy-start | bytes 196612
Sparse Core Ops, SparseCore 0:
  426.2 79.1 all-reduce.4
where the time goes:
time: 515 us; the launch traced here: 514 us
  blocking collectives  279 us (54%)
  local copies, waits for them, and re-layouts  95.7 us (19%)
  waiting for transfers between devices  53.5 us (10%)
  matrix products  48.8 us (9%)
  other arithmetic  15.6 us (3%)
  between operations  15.4 us (3%)
  starting transfers between devices  5.18 us (1%)
    all_gather x1, blocking collectives, body(): row_vectors = lax.all_gather(trial, 'kc', axis=0, tiled=True)  224 us
    unnamed x2, waiting for transfers between devices  53.5 us
    unnamed x2, blocking collectives  42.1 us
    unnamed x19, local copies, waits for them, and re-layouts  25.5 us
    all_to_all x1, local copies, waits for them, and re-layouts, body(): lax.all_to_all(outgoing, 'kc', split_axis=0, concat_axis=3, tiled=True)[0]  22.4 us
    unnamed x1, matrix products  21.5 us
    reshape x3, local copies, waits for them, and re-layouts, body(): direct_kernel = direct_kernel.reshape(pair_total, NCON, NCON, NVAL, NVAL)  19.3 us
    select_n x2, other arithmetic, body(): jnp.take(screened, wanted, axis=0)  14.2 us
  transfers between devices with their start and end apart: 2, of which 1 were waited for; matrix products, arithmetic and copies ran while one was open for 7% of the time, Pallas kernels for 0%

commit v1 on v0

v1 whole, which is shorter than its diff:
```python
import functools

import jax
import jax.numpy as jnp
from jax import lax
from jax.experimental import pallas as pl
from jax.experimental.pallas import tpu as pltpu
from jax.sharding import PartitionSpec as P

MESH = pl.DeviceIdType.MESH
F32 = jnp.float32
BF = jnp.bfloat16
NU = 8
NC = 4
RC = 64
PLANE_ROWS = 1024

SEQ = (
    "S00", "S01", "S10", "T00", "P0", "S20", "S11", "P1", "S02", "S30",
    "M0", "P2", "S21", "S12", "S03", "P3", "S40", "S31", "S22", "S13",
    "T01", "P4", "S41", "S32", "S23", "T10", "P5", "S42", "S33", "T20",
    "T11", "T02", "P6", "S43", "P7", "T21", "T12", "T03", "X0", "Y0",
    "C0", "T22", "C1", "T13", "E0", "T23", "C2", "E1", "C3", "E2",
    "E3",
)


def kernel(w, dens, mom, count, rows, cols, trial, out, momv, moml, moms, *scratch):
    ag_b, ag_1, ag_2 = scratch[:NU], scratch[NU:NU + NC], scratch[NU + NC:NU + 2 * NC]
    (
        st_b, land_b, land_1, land_2,
        rv, rcd, kacc, xr, xc, xf, br, bc, pick_r, pick_c, kd, sum_r, sum_c, land_r, land_c,
        msend, mrecv, bsend, brecv, dsend, drecv, asend, arecv, xsend, xrecv, ysend, yrecv, lsem, psem,
    ) = scratch[NU + 2 * NC:]
    kr = lax.axis_index("kr")
    kc = lax.axis_index("kc")
    z, c, y, x = kr // 2, kr % 2, kc // 4, kc % 4

    def dev(x_, y_, z_, c_):
        return (z_ * 2 + c_, y_ * 4 + x_)

    def member(g, d):
        a, cc = d // 2, d % 2
        return (dev(x, y, a, cc), dev(a, y, z, cc), dev(x, a, z, cc))[g]

    mine = (z * 2 + c, x * 2 + c, y * 2 + c)
    xp, xm, yp, ym = (x + 1) % 4, (x + 3) % 4, (y + 1) % 4, (y + 3) % 4
    to_x = (dev(xp, y, z, c), dev(xm, y, z, c))
    to_y = (dev(x, yp, z, c), dev(x, ym, z, c))

    def copy_to(src, dst, ss, rs, to):
        return pltpu.make_async_remote_copy(
            src_ref=src, dst_ref=dst, send_sem=ss, recv_sem=rs, device_id=to, device_id_type=MESH
        )

    sent = []
    left = set()

    def go(copies):
        for cp in copies:
            cp.start()
            sent.append(cp)
        return copies

    def local(src, dst, sem):
        cp = pltpu.make_async_copy(src, dst, sem)
        cp.start()
        return cp

    def rows_b(u):
        return pl.ds(pl.multiple_of(kr * (NU * 16) + u * 16, 16), 16)

    def rows_d(p, h):
        return pl.ds(pl.multiple_of(PLANE_ROWS + p * 512 + c * 256 + h * RC, 16), RC)

    own_b = [local(w.at[:, rows_b(u)], ag_b[u].at[y, x], lsem.at[u]) for u in range(NU)]
    own_d = [
        [local(w.at[:, rows_d(0, h)], ag_1[h].at[y], lsem.at[NU + h]) for h in range(NC)],
        [local(w.at[:, rows_d(1, h)], ag_2[h].at[x], lsem.at[NU + NC + h]) for h in range(NC)],
    ]
    dens_in = []
    for b in range(8):
        for half in range(2):
            pair = (b * 2 + half) * 2
            lanes = pl.ds(half * 128, 128)
            dens_in.append((
                local(dens.at[pair], rcd.at[b, :, :, lanes], psem.at[pair]),
                local(dens.at[pair + 1], rv.at[b, :, :, lanes], psem.at[pair + 1]),
            ))

    bar = pltpu.get_barrier_semaphore()
    greet = [member(g, (mine[g] + k) % 8) for g in range(3) for k in range(1, 8)]
    greet += [dev((x + dx) % 4, (y + dy) % 4, z, c) for dy in range(1, 4) for dx in range(1, 4)]
    for to in greet:
        pl.semaphore_signal(bar, 1, device_id=to, device_id_type=MESH)
    lane8 = lax.broadcasted_iota(jnp.int32, (8, 128), 1)
    momv[...] = jnp.where(lane8 == 0, mom[0], mom[1])
    for g in range(3):
        moml[g, mine[g]] = momv[...]
    kacc[...] = jnp.zeros_like(kacc)
    pl.semaphore_wait(bar, len(greet))

    mom_out = []
    for g in range(3):
        for k in range(1, 8):
            mom_out.append(copy_to(
                momv, moml.at[g, mine[g]], msend.at[g, k - 1], mrecv.at[g, k - 1], member(g, (mine[g] + k) % 8)
            ))

    trial_out = []
    for k in range(1, 16):
        trial_out.append(copy_to(trial, xr.at[kc], xsend.at[k - 1], xrecv.at[k - 1], (kr, (kc + k) % 16)))
    for k in range(1, 8):
        trial_out.append(copy_to(trial, xc.at[kr], xsend.at[14 + k], xrecv.at[14 + k], ((kr + k) % 8, kc)))

    flow = {}

    def b_copy(u, i, src, dst, to):
        return copy_to(src, dst, bsend.at[u, i], brecv.at[u, i], to)

    def s0(u):
        own_b[u].wait()
        own = ag_b[u].at[y, x]
        to = (to_x, to_y)[u % 2]
        flow[u, 0] = go([b_copy(u, i, own, own, to[i]) for i in range(2)])

    def s1(u):
        for cp in flow[u, 0]:
            cp.wait_recv()
        if u % 2 == 0:
            a, b, to = ag_b[u].at[y, xm, 0:8], ag_b[u].at[y, xp, 8:16], to_x
        else:
            a, b, to = ag_b[u].at[ym, x, 0:8], ag_b[u].at[yp, x, 8:16], to_y
        flow[u, 1] = go([b_copy(u, 2, a, a, to[0]), b_copy(u, 3, b, b, to[1])])

    def s2(u):
        for cp in flow[u, 1]:
            cp.wait_recv()
        line, to = (ag_b[u].at[y], to_y) if u % 2 == 0 else (ag_b[u].at[:, x], to_x)
        flow[u, 2] = go([b_copy(u, 4, line, line, to[0]), b_copy(u, 5, line, line, to[1])])

    def s3(u):
        for cp in flow[u, 2]:
            cp.wait_recv()
        if u % 2 == 0:
            a, b, to = ag_b[u].at[ym, 0:2], ag_b[u].at[yp, 2:4], to_y
        else:
            a, b, to = ag_b[u].at[0:2, xm], ag_b[u].at[2:4, xp], to_x
        flow[u, 3] = go([b_copy(u, 6, a, a, to[0]), b_copy(u, 7, b, b, to[1])])

    arrive_b = [[] for _ in range(NU)]
    arrive_d = [[] for _ in range(NC)]

    def s4(u):
        for cp in flow[u, 3]:
            cp.wait_recv()
        me = mine[0]
        for k in range(1, 8):
            d = (me + k) % 8
            for s in range(2):
                st_b[u, k - 1, s] = ag_b[u][:, :, moms[0, d, 0, s]].reshape(16, 16, 128)
            arrive_b[u] += go([copy_to(
                st_b.at[u, k - 1], land_b.at[me, u], asend.at[u, k - 1], arecv.at[u, k - 1], member(0, d)
            )])
        for s in range(2):
            land_b[me, u, s] = ag_b[u][:, :, moms[0, me, 0, s]].reshape(16, 16, 128)

    def t0(h):
        for p, (ag, pos, to) in enumerate(((ag_1, y, to_y), (ag_2, x, to_x))):
            own_d[p][h].wait()
            own = ag[h].at[pos]
            flow[p, h, 0] = go([copy_to(own, own, dsend.at[p, h, i], drecv.at[p, h, i], to[i]) for i in range(2)])

    def t1(h):
        for p, (ag, m, q, to) in enumerate(((ag_1, ym, yp, to_y), (ag_2, xm, xp, to_x))):
            for cp in flow[p, h, 0]:
                cp.wait_recv()
            a, b = ag[h].at[m, 0:8], ag[h].at[q, 8:16]
            flow[p, h, 1] = go([
                copy_to(a, a, dsend.at[p, h, 2], drecv.at[p, h, 2], to[0]),
                copy_to(b, b, dsend.at[p, h, 3], drecv.at[p, h, 3], to[1]),
            ])

    def t2(h):
        for p, (ag, land) in enumerate(((ag_1, land_1), (ag_2, land_2))):
            for cp in flow[p, h, 1]:
                cp.wait_recv()
            u = p * NC + h
            for stage in range(4):
                for cp in flow[u, stage]:
                    cp.wait_send()
                    left.add(id(cp))
            me = mine[1 + p]
            for k in range(1, 8):
                d = (me + k) % 8
                place = ag_b[u].at[(k - 1) // 2, pl.ds(2 * ((k - 1) % 2), 2)]
                for s in range(2):
                    place[s] = ag[h][:, moms[1 + p, d, 0, s]].reshape(16, 16, 128)
                arrive_d[h] += go([copy_to(
                    place, land.at[me, h], asend.at[NU + u, k - 1], arecv.at[NU + u, k - 1], member(1 + p, d)
                )])
            for s in range(2):
                land[me, h, s] = ag[h][:, moms[1 + p, me, 0, s]].reshape(16, 16, 128)

    def m0():
        for cp in mom_out:
            cp.wait()
        cp = pltpu.make_async_copy(moml, moms, lsem.at[NU + 2 * NC])
        cp.start()
        cp.wait()

    def pack(b):
        for half in range(2):
            for cp in dens_in[b * 2 + half]:
                cp.wait()

        @pl.loop(0, 16)
        def _(i):
            for half in range(2):
                lanes = pl.ds(half * 128, 128)
                a = rcd[b, i, :, lanes]
                v = rv[b, i, :, lanes]
                low = lax.broadcasted_iota(jnp.int32, (128, 128), 1) < 64
                rcd[b, i, :, lanes] = jnp.where(low, a, pltpu.roll(v, 64, 1))
                rv[b, i, :, lanes] = jnp.where(low, pltpu.roll(a, 64, 1), v)

    def multiply(load_w, load_c):
        def gather(b, val):
            for half in range(2):
                lanes = slice(half * 128, half * 128 + 128)
                kacc[b * 2 + half] += lax.dot_general(
                    load_c(b, lanes), val[:, lanes], (((0,), (0,)), ((), ())), preferred_element_type=F32
                )

        before = None
        for b in range(8):
            if b % 4 == 0:
                lhs = load_w(b // 4)
            val = jnp.dot(lhs, rv[b].reshape(2048, 256), preferred_element_type=F32).astype(BF)
            if before is not None:
                gather(b - 1, before)
            before = val
        gather(7, before)

    def c_step(t):
        for u in (2 * t, 2 * t + 1):
            for cp in arrive_b[u]:
                cp.wait_recv()

        def load_w(s):
            return jnp.concatenate(
                [land_b[:, 2 * t:2 * t + 2, s, j].reshape(256, 128) for j in range(16)], axis=1
            )

        def load_c(b, lanes):
            return rcd[b, 0:8, 32 * t:32 * t + 32, lanes].reshape(256, 128)

        multiply(load_w, load_c)

    def e_step(h):
        for cp in arrive_d[h]:
            cp.wait_recv()

        def load_w(s):
            parts = []
            for j in range(16):
                yy, xx = j // 4, j % 4
                parts.append(jnp.concatenate(
                    [land_1[xx * 2 + cc, h, s, 4 * yy:4 * yy + 4].reshape(64, 128) for cc in range(2)]
                    + [land_2[yy * 2 + cc, h, s, 4 * xx:4 * xx + 4].reshape(64, 128) for cc in range(2)],
                    axis=0,
                ))
            return jnp.concatenate(parts, axis=1)

        def load_c(b, lanes):
            part = slice((h % 2) * 64, (h % 2) * 64 + 64)
            return jnp.concatenate([rcd[b, 8 + 2 * i + h // 2, part, lanes] for i in range(4)], axis=0)

        multiply(load_w, load_c)

    def x_step():
        for cp in trial_out:
            cp.wait()
        xr[kc] = trial[...]
        xc[kr] = trial[...]
        low = lax.broadcasted_iota(jnp.int32, (8, 128), 1) < 64
        src = lax.broadcasted_iota(jnp.int32, (128, 1024), 0)
        dst = lax.broadcasted_iota(jnp.int32, (128, 1024), 1)
        n, p2, v, vv = dst // 128, (dst // 64) % 2, (dst // 8) % 8, dst % 8
        for land, size, pairs, table, band in ((xr, 16, rows, bc, v), (xc, 8, cols, br, vv)):
            xf[0:size * 2] = land[...].astype(F32).reshape(size * 2, 8, 128)
            spread = (src == p2 * 64 + band * 8 + n).astype(F32)
            for pp in range(16):
                first = xf[pairs[2 * pp]]
                second = xf[pairs[2 * pp + 1]]
                both = jnp.where(low, first, second)
                table[pp] = jnp.dot(both, spread, preferred_element_type=F32)

    def y_step():
        lane = lax.broadcasted_iota(jnp.int32, (1, 128), 1)
        for pp in range(16):
            for pairs, band, table, size in ((rows, (lane // 8) % 8, pick_r, 256), (cols, lane % 8, pick_c, 128)):
                p = 2 * pp
                place = jnp.where(lane < 64, pairs[p], pairs[p + 1])
                listed = jnp.where(lane < 64, p % 16, p % 16 + 1) < count[p // 16]
                key = jnp.where(listed, place * 8 + band, -1)
                at = lax.broadcasted_iota(jnp.int32, (size, 128), 0)
                table[pp] = (at == key).astype(F32).astype(BF)

    def finish():
        sum_r[...] = jnp.zeros_like(sum_r)
        sum_c[...] = jnp.zeros_like(sum_c)

        @pl.loop(0, 16)
        def _(pp):
            low = lax.broadcasted_iota(jnp.int32, (64, 128), 1) < 64
            kd[...] = jnp.where(low, kacc[pp, 0:64], kacc[pp, 64:128])
            by_row = [kd[pl.ds(i, 8, stride=8)] for i in range(8)]
            by_col = [kd[8 * i:8 * i + 8] for i in range(8)]
            for table, pieces, pick, total in ((br, by_row, pick_r, sum_r), (bc, by_col, pick_c, sum_c)):
                parts = []
                for n in range(8):
                    lanes = slice(n * 128, n * 128 + 128)
                    parts.append(sum(pieces[i] * table[pp, i:i + 1, lanes] for i in range(8)))
                whole = jnp.concatenate(parts, axis=0)
                high = whole.astype(BF)
                rest = (whole - high.astype(F32)).astype(BF)
                total[...] += lax.dot_general(
                    pick[pp], jnp.concatenate([high, rest], axis=0), (((1,), (1,)), ((), ())),
                    preferred_element_type=F32,
                )

        last = []
        for k in range(1, 16):
            d = (kc + k) % 16
            last.append(copy_to(
                sum_r.at[pl.ds(pl.multiple_of(d * 16, 16), 16)], land_r.at[kc],
                ysend.at[k - 1], yrecv.at[k - 1], (kr, d),
            ))
        for k in range(1, 8):
            d = (kr + k) % 8
            last.append(copy_to(
                sum_c.at[pl.ds(pl.multiple_of(d * 16, 16), 16)], land_c.at[kr],
                ysend.at[14 + k], yrecv.at[14 + k], (d, kc),
            ))
        for cp in last:
            cp.start()
        land_r[kc] = sum_r[pl.ds(pl.multiple_of(kc * 16, 16), 16)]
        land_c[kr] = sum_c[pl.ds(pl.multiple_of(kr * 16, 16), 16)]
        for cp in last:
            cp.wait()
        total = land_r[0] + land_c[0]
        for i in range(1, 16):
            total += land_r[i]
        for i in range(1, 8):
            total += land_c[i]
        out[...] = total

    for cp in mom_out:
        cp.start()
    started = False
    steps = {"S0": s0, "S1": s1, "S2": s2, "S3": s3, "S4": s4, "T0": t0, "T1": t1, "T2": t2}
    for step in SEQ:
        i = int(step[-1])
        if step[0] == "S":
            steps[step[:2]](2 * i)
            steps[step[:2]](2 * i + 1)
        elif step[0] == "T":
            steps[step[:2]](i)
        elif step[0] == "M":
            m0()
            for cp in trial_out:
                cp.start()
        elif step[0] == "P":
            pack(i)
        elif step[0] == "X":
            x_step()
        elif step[0] == "Y":
            y_step()
        elif step[0] == "C":
            c_step(i)
        elif step[0] == "E":
            e_step(i)
    finish()
    for cp in sent:
        if id(cp) not in left:
            cp.wait_send()


def body(trial, screened, density, pair_rows, pair_cols, slot_momentum, slot_count):
    half = trial.reshape(16, 64)
    doubled = jnp.concatenate([half, half], axis=1)
    smem = pl.BlockSpec(memory_space=pltpu.SMEM)
    anywhere = pl.BlockSpec(memory_space=pl.ANY)
    vmem = pl.BlockSpec(memory_space=pltpu.VMEM)
    dma = pltpu.SemaphoreType.DMA
    total = pl.pallas_call(
        kernel,
        out_shape=jax.ShapeDtypeStruct((16, 128), F32),
        in_specs=[anywhere, anywhere, smem, smem, smem, smem, vmem],
        out_specs=vmem,
        scratch_shapes=[
            pltpu.VMEM((8, 128), jnp.int32),
            pltpu.VMEM((3, 8, 8, 128), jnp.int32),
            pltpu.SMEM((3, 8, 8, 128), jnp.int32),
            *[pltpu.VMEM((4, 4, 16, 16, 128), BF)] * NU,
            *[pltpu.VMEM((4, 16, RC, 128), BF)] * (2 * NC),
            pltpu.VMEM((NU, 7, 2, 16, 16, 128), BF),
            pltpu.VMEM((8, NU, 2, 16, 16, 128), BF),
            pltpu.VMEM((8, NC, 2, 16, 16, 128), BF),
            pltpu.VMEM((8, NC, 2, 16, 16, 128), BF),
            pltpu.VMEM((8, 16, 128, 256), BF),
            pltpu.VMEM((8, 16, 128, 256), BF),
            pltpu.VMEM((16, 128, 128), F32),
            pltpu.VMEM((16, 16, 128), BF),
            pltpu.VMEM((8, 16, 128), BF),
            pltpu.VMEM((32, 8, 128), F32),
            pltpu.VMEM((16, 8, 1024), F32),
            pltpu.VMEM((16, 8, 1024), F32),
            pltpu.VMEM((16, 256, 128), BF),
            pltpu.VMEM((16, 128, 128), BF),
            pltpu.VMEM((64, 128), F32),
            pltpu.VMEM((256, 128), F32),
            pltpu.VMEM((128, 128), F32),
            pltpu.VMEM((16, 16, 128), F32),
            pltpu.VMEM((8, 16, 128), F32),
            dma((3, 7)), dma((3, 7)), dma((NU, 8)), dma((NU, 8)), dma((2, NC, 4)), dma((2, NC, 4)),
            dma((NU + 2 * NC, 7)), dma((NU + 2 * NC, 7)), dma((22,)), dma((22,)), dma((22,)), dma((22,)),
            dma((NU + 2 * NC + 1,)), dma((32,)),
        ],
        compiler_params=pltpu.CompilerParams(
            collective_id=0, has_side_effects=True, vmem_limit_bytes=62 * 2**20
        ),
    )(
        screened, density.reshape(density.shape[0], 16, 128, 128),
        slot_momentum, slot_count, pair_rows, pair_cols, doubled,
    )
    total = total.reshape(2, 8, 2, 8, 8)
    total = total[:, :, 0] + total[:, :, 1]
    return total.transpose(0, 3, 1, 2).reshape(2, 512)


def solution(mesh):
    return jax.shard_map(
        body,
        mesh=mesh,
        in_specs=(
            P(("kr", "kc"), None),
            P(None, None, "kc"),
            P(("kr", "kc"), None, None),
            P(("kr", "kc")),
            P(("kr", "kc")),
            P(("kr", "kc")),
            P(("kr", "kc")),
        ),
        out_specs=P(("kr", "kc"), None),
        check_vma=False,
    )
```

time: 515 us -> 163 us (0.32)
  blocking collectives: 279 us -> 0 us
  Pallas kernels: 0 us -> 159 us
  local copies, waits for them, and re-layouts: 95.7 us -> 2.34 us
  waiting for transfers between devices: 53.5 us -> 0 us
  matrix products: 48.8 us -> 0 us
  between operations: 15.4 us -> 0.03 us
  other arithmetic: 15.6 us -> 0.68 us
  starting transfers between devices: 5.18 us -> 0 us
    all_gather x2 -> x0, blocking collectives: 237 us -> none  [the longest x1 224 us: body(): row_vectors = lax.all_gather(trial, 'kc', axis=0, tiled=True)]
    pallas_call x0 -> x1, Pallas kernels: none -> 159 us  [body(): pl.pallas_call(kernel, out_shape=jax.ShapeDtypeStruct((16, 128), F32), in...]
    unnamed x2 -> x0, waiting for transfers between devices: 53.5 us -> none
    unnamed x2 -> x0, blocking collectives: 42.1 us -> none
    dot_general x7 -> x0, matrix products: 27.3 us -> none  [the longest x1 11.4 us: body(): jnp.einsum('pcdvw,pdwn->pcvn', direct_kernel, vec_col, precision=high)]
    unnamed x19 -> x0, local copies, waits for them, and re-layouts: 25.5 us -> none
    all_to_all x1 -> x0, local copies, waits for them, and re-layouts: 22.4 us -> none  [body(): lax.all_to_all(outgoing, 'kc', split_axis=0, concat_axis=3, tiled=True)[0]]
    unnamed x1 -> x0, matrix products: 21.5 us -> none
  transfers between devices with their start and end apart: 2 -> 0, of which waited for: 1 -> 0; matrix products, arithmetic and copies ran while one was open for 7% -> 0% of each run, Pallas kernels for 0% -> 0%
where the time goes in v1:
time: 163 us; the launch traced here: 162 us
  Pallas kernels  159 us (98%)
  local copies, waits for them, and re-layouts  2.34 us (1%)
    pallas_call x1, Pallas kernels, body(): pl.pallas_call(kernel, out_shape=jax.ShapeDtypeStruct((16, 128), F32), in...  159 us

profile of v1, /device:TPU:0, one launch (start us, length us, event | category | flops | bytes accessed | tf_op | source)
XLA Modules:
  0.0 162.4 jit_solution(9467636358080049762)
XLA Ops:
  0.0 0.8 reshape.14
  0.8 0.7 pad_maximum_fusion.trial
  1.4 159.4 %shard_map.73 = f32[16,128]{1,0:T(8,128)} custom-call(bf16[16,2048,128]{2,1,0:T(8,128)(2,1)} %w.1, bf16[32,16,128,128]{3,2,1,0:T(8,128)(2,1)} %bitcast.7, s32[2]{0:T(128)} %mom.1, s32[2]{0:T(128)} %count.1, s32[32]{0:T(128)} %rows.1, s32[32]{0:T(128)} %cols.1, bf16[16,128]{1,0:T(8,128)(2,1)} %pad_maximum_fusion.trial), custom_call_target="tpu_custom_call" | custom-call | tf_op jit(solution)/shard_map/pallas_call | solution.py:397
  160.8 0.8 reshape.15
  161.6 0.1 copy.8
  161.7 0.7 reshape.16
  (1 shorter events, 0.0 us)

commit v2 on v1

--- a/solution.py
+++ b/solution.py
@@ -16,12 +16,13 @@
 PLANE_ROWS = 1024
 
 SEQ = (
-    "S00", "S01", "S10", "T00", "P0", "S20", "S11", "P1", "S02", "S30",
-    "M0", "P2", "S21", "S12", "S03", "P3", "S40", "S31", "S22", "S13",
-    "T01", "P4", "S41", "S32", "S23", "T10", "P5", "S42", "S33", "T20",
-    "T11", "T02", "P6", "S43", "P7", "T21", "T12", "T03", "X0", "Y0",
-    "C0", "T22", "C1", "T13", "E0", "T23", "C2", "E1", "C3", "E2",
-    "E3",
+    "S00", "T000", "S02", "S05", "S01", "S03", "L0", "N0", "S06", "S10", "S07", "S04", "T012", "P0",
+    "S12", "S11", "S15", "T010", "S20", "S21", "S13", "T100", "S30", "T001", "S16", "T110",
+    "M0", "S22", "S17", "S31", "T011", "S14", "S23", "S40", "T101", "S41", "P5", "P7",
+    "P6", "S32", "S24", "P1", "S27", "P2", "S25", "P4", "S33", "T210", "S42", "S34",
+    "T013", "S35", "P3", "T200", "T003", "S26", "S43", "S45", "X0", "Y0", "T103", "T111",
+    "T113", "T002", "S44", "T112", "S36", "S37", "T201", "T211", "C0", "T102", "T213", "T203",
+    "E0", "S47", "S46", "C1", "E1", "T202", "C2", "T212", "E3", "C3", "E2",
 )
 
 
@@ -62,6 +63,12 @@
             sent.append(cp)
         return copies
 
+    bar = pltpu.get_barrier_semaphore()
+    greet = [member(g, (mine[g] + k) % 8) for g in range(3) for k in range(1, 8)]
+    greet += [dev((x + dx) % 4, (y + dy) % 4, z, c) for dy in range(1, 4) for dx in range(1, 4)]
+    for to in greet:
+        pl.semaphore_signal(bar, 1, device_id=to, device_id_type=MESH)
+
     def local(src, dst, sem):
         cp = pltpu.make_async_copy(src, dst, sem)
         cp.start()
@@ -79,20 +86,17 @@
         [local(w.at[:, rows_d(1, h)], ag_2[h].at[x], lsem.at[NU + NC + h]) for h in range(NC)],
     ]
     dens_in = []
-    for b in range(8):
-        for half in range(2):
-            pair = (b * 2 + half) * 2
-            lanes = pl.ds(half * 128, 128)
-            dens_in.append((
-                local(dens.at[pair], rcd.at[b, :, :, lanes], psem.at[pair]),
-                local(dens.at[pair + 1], rv.at[b, :, :, lanes], psem.at[pair + 1]),
-            ))
-
-    bar = pltpu.get_barrier_semaphore()
-    greet = [member(g, (mine[g] + k) % 8) for g in range(3) for k in range(1, 8)]
-    greet += [dev((x + dx) % 4, (y + dy) % 4, z, c) for dy in range(1, 4) for dx in range(1, 4)]
-    for to in greet:
-        pl.semaphore_signal(bar, 1, device_id=to, device_id_type=MESH)
+
+    def load():
+        for b in range(8):
+            for half in range(2):
+                pair = (b * 2 + half) * 2
+                lanes = pl.ds(half * 128, 128)
+                dens_in.append((
+                    local(dens.at[pair], rcd.at[b, :, :, lanes], psem.at[pair]),
+                    local(dens.at[pair + 1], rv.at[b, :, :, lanes], psem.at[pair + 1]),
+                ))
+
     lane8 = lax.broadcasted_iota(jnp.int32, (8, 128), 1)
     momv[...] = jnp.where(lane8 == 0, mom[0], mom[1])
     for g in range(3):
@@ -148,6 +152,7 @@
             a, b, to = ag_b[u].at[0:2, xm], ag_b[u].at[2:4, xp], to_x
         flow[u, 3] = go([b_copy(u, 6, a, a, to[0]), b_copy(u, 7, b, b, to[1])])
 
+    free_units = []
     arrive_b = [[] for _ in range(NU)]
     arrive_d = [[] for _ in range(NC)]
 
@@ -164,43 +169,45 @@
             )])
         for s in range(2):
             land_b[me, u, s] = ag_b[u][:, :, moms[0, me, 0, s]].reshape(16, 16, 128)
-
-    def t0(h):
-        for p, (ag, pos, to) in enumerate(((ag_1, y, to_y), (ag_2, x, to_x))):
-            own_d[p][h].wait()
-            own = ag[h].at[pos]
-            flow[p, h, 0] = go([copy_to(own, own, dsend.at[p, h, i], drecv.at[p, h, i], to[i]) for i in range(2)])
-
-    def t1(h):
-        for p, (ag, m, q, to) in enumerate(((ag_1, ym, yp, to_y), (ag_2, xm, xp, to_x))):
-            for cp in flow[p, h, 0]:
-                cp.wait_recv()
-            a, b = ag[h].at[m, 0:8], ag[h].at[q, 8:16]
-            flow[p, h, 1] = go([
-                copy_to(a, a, dsend.at[p, h, 2], drecv.at[p, h, 2], to[0]),
-                copy_to(b, b, dsend.at[p, h, 3], drecv.at[p, h, 3], to[1]),
-            ])
-
-    def t2(h):
-        for p, (ag, land) in enumerate(((ag_1, land_1), (ag_2, land_2))):
-            for cp in flow[p, h, 1]:
-                cp.wait_recv()
-            u = p * NC + h
-            for stage in range(4):
-                for cp in flow[u, stage]:
-                    cp.wait_send()
-                    left.add(id(cp))
-            me = mine[1 + p]
-            for k in range(1, 8):
-                d = (me + k) % 8
-                place = ag_b[u].at[(k - 1) // 2, pl.ds(2 * ((k - 1) % 2), 2)]
-                for s in range(2):
-                    place[s] = ag[h][:, moms[1 + p, d, 0, s]].reshape(16, 16, 128)
-                arrive_d[h] += go([copy_to(
-                    place, land.at[me, h], asend.at[NU + u, k - 1], arecv.at[NU + u, k - 1], member(1 + p, d)
-                )])
+        free_units.append(u)
+
+    def t0(p, h):
+        ag, pos, to = ((ag_1, y, to_y), (ag_2, x, to_x))[p]
+        own_d[p][h].wait()
+        own = ag[h].at[pos]
+        flow[p, h, 0] = go([copy_to(own, own, dsend.at[p, h, i], drecv.at[p, h, i], to[i]) for i in range(2)])
+
+    def t1(p, h):
+        ag, m, q, to = ((ag_1, ym, yp, to_y), (ag_2, xm, xp, to_x))[p]
+        for cp in flow[p, h, 0]:
+            cp.wait_recv()
+        a, b = ag[h].at[m, 0:8], ag[h].at[q, 8:16]
+        flow[p, h, 1] = go([
+            copy_to(a, a, dsend.at[p, h, 2], drecv.at[p, h, 2], to[0]),
+            copy_to(b, b, dsend.at[p, h, 3], drecv.at[p, h, 3], to[1]),
+        ])
+
+    def t2(p, h):
+        ag, land = ((ag_1, land_1), (ag_2, land_2))[p]
+        for cp in flow[p, h, 1]:
+            cp.wait_recv()
+        u = free_units.pop(0)
+        r = NU + p * NC + h
+        for stage in range(4):
+            for cp in flow[u, stage]:
+                cp.wait_send()
+                left.add(id(cp))
+        me = mine[1 + p]
+        for k in range(1, 8):
+            d = (me + k) % 8
+            place = ag_b[u].at[(k - 1) // 2, pl.ds(2 * ((k - 1) % 2), 2)]
             for s in range(2):
-                land[me, h, s] = ag[h][:, moms[1 + p, me, 0, s]].reshape(16, 16, 128)
+                place[s] = ag[h][:, moms[1 + p, d, 0, s]].reshape(16, 16, 128)
+            arrive_d[h] += go([copy_to(
+                place, land.at[me, h], asend.at[r, k - 1], arecv.at[r, k - 1], member(1 + p, d)
+            )])
+        for s in range(2):
+            land[me, h, s] = ag[h][:, moms[1 + p, me, 0, s]].reshape(16, 16, 128)
 
     def m0():
         for cp in mom_out:
@@ -214,15 +221,16 @@
             for cp in dens_in[b * 2 + half]:
                 cp.wait()
 
-        @pl.loop(0, 16)
+        @pl.loop(0, 4)
         def _(i):
+            part = pl.ds(i * 4, 4)
             for half in range(2):
                 lanes = pl.ds(half * 128, 128)
-                a = rcd[b, i, :, lanes]
-                v = rv[b, i, :, lanes]
-                low = lax.broadcasted_iota(jnp.int32, (128, 128), 1) < 64
-                rcd[b, i, :, lanes] = jnp.where(low, a, pltpu.roll(v, 64, 1))
-                rv[b, i, :, lanes] = jnp.where(low, pltpu.roll(a, 64, 1), v)
+                a = rcd[b, part, :, lanes].reshape(512, 128)
+                v = pltpu.roll(rv[b, part, :, lanes].reshape(512, 128), 64, 1)
+                low = lax.broadcasted_iota(jnp.int32, (512, 128), 1) < 64
+                rcd[b, part, :, lanes] = jnp.where(low, a, v).reshape(4, 128, 128)
+                rv[b, part, :, lanes] = jnp.where(low, v, a).reshape(4, 128, 128)
 
     def multiply(load_w, load_c):
         def gather(b, val):
@@ -232,15 +240,17 @@
                     load_c(b, lanes), val[:, lanes], (((0,), (0,)), ((), ())), preferred_element_type=F32
                 )
 
-        before = None
-        for b in range(8):
-            if b % 4 == 0:
-                lhs = load_w(b // 4)
-            val = jnp.dot(lhs, rv[b].reshape(2048, 256), preferred_element_type=F32).astype(BF)
-            if before is not None:
-                gather(b - 1, before)
-            before = val
-        gather(7, before)
+        @pl.loop(0, 2)
+        def _(s):
+            lhs = load_w(s)
+            before = None
+            for i in range(4):
+                b = s * 4 + i
+                val = jnp.dot(lhs, rv[b].reshape(2048, 256), preferred_element_type=F32).astype(BF)
+                if before is not None:
+                    gather(b - 1, before)
+                before = val
+            gather(s * 4 + 3, before)
 
     def c_step(t):
         for u in (2 * t, 2 * t + 1):
@@ -290,19 +300,24 @@
         for land, size, pairs, table, band in ((xr, 16, rows, bc, v), (xc, 8, cols, br, vv)):
             xf[0:size * 2] = land[...].astype(F32).reshape(size * 2, 8, 128)
             spread = (src == p2 * 64 + band * 8 + n).astype(F32)
-            for pp in range(16):
-                first = xf[pairs[2 * pp]]
-                second = xf[pairs[2 * pp + 1]]
-                both = jnp.where(low, first, second)
-                table[pp] = jnp.dot(both, spread, preferred_element_type=F32)
+
+            @pl.loop(0, 4)
+            def _(g):
+                both = [
+                    jnp.where(low, xf[pairs[8 * g + 2 * j + 1]], xf[pairs[8 * g + 2 * j]]) for j in range(4)
+                ]
+                wide = jnp.dot(jnp.concatenate(both, axis=0), spread, preferred_element_type=F32)
+                table[pl.ds(g * 4, 4)] = wide.reshape(4, 8, 1024)
 
     def y_step():
         lane = lax.broadcasted_iota(jnp.int32, (1, 128), 1)
-        for pp in range(16):
+
+        @pl.loop(0, 16)
+        def _(pp):
+            p = 2 * pp
+            listed = jnp.where(lane < 64, (p + 1) % 16, p % 16) < count[pp // 8]
             for pairs, band, table, size in ((rows, (lane // 8) % 8, pick_r, 256), (cols, lane % 8, pick_c, 128)):
-                p = 2 * pp
-                place = jnp.where(lane < 64, pairs[p], pairs[p + 1])
-                listed = jnp.where(lane < 64, p % 16, p % 16 + 1) < count[p // 16]
+                place = jnp.where(lane < 64, pairs[p + 1], pairs[p])
                 key = jnp.where(listed, place * 8 + band, -1)
                 at = lax.broadcasted_iota(jnp.int32, (size, 128), 0)
                 table[pp] = (at == key).astype(F32).astype(BF)
@@ -311,13 +326,12 @@
         sum_r[...] = jnp.zeros_like(sum_r)
         sum_c[...] = jnp.zeros_like(sum_c)
 
-        @pl.loop(0, 16)
-        def _(pp):
+        def apply(pp, slot):
             low = lax.broadcasted_iota(jnp.int32, (64, 128), 1) < 64
-            kd[...] = jnp.where(low, kacc[pp, 0:64], kacc[pp, 64:128])
-            by_row = [kd[pl.ds(i, 8, stride=8)] for i in range(8)]
-            by_col = [kd[8 * i:8 * i + 8] for i in range(8)]
-            for table, pieces, pick, total in ((br, by_row, pick_r, sum_r), (bc, by_col, pick_c, sum_c)):
+            kd[slot] = jnp.where(low, kacc[pp, 64:128], kacc[pp, 0:64])
+            by_row = [kd[slot, pl.ds(i, 8, stride=8)] for i in range(8)]
+            by_col = [kd[slot, 8 * i:8 * i + 8] for i in range(8)]
+            for table, pieces in ((br, by_row), (bc, by_col)):
                 parts = []
                 for n in range(8):
                     lanes = slice(n * 128, n * 128 + 128)
@@ -325,9 +339,16 @@
                 whole = jnp.concatenate(parts, axis=0)
                 high = whole.astype(BF)
                 rest = (whole - high.astype(F32)).astype(BF)
+                yield jnp.concatenate([high, rest], axis=0)
+
+        @pl.loop(0, 4)
+        def _(g):
+            both = [tuple(apply(g * 4 + j, j)) for j in range(4)]
+            for i, (pick, total) in enumerate(((pick_r, sum_r), (pick_c, sum_c))):
                 total[...] += lax.dot_general(
-                    pick[pp], jnp.concatenate([high, rest], axis=0), (((1,), (1,)), ((), ())),
-                    preferred_element_type=F32,
+                    jnp.concatenate([pick[g * 4 + j] for j in range(4)], axis=1),
+                    jnp.concatenate([pair[i] for pair in both], axis=1),
+                    (((1,), (1,)), ((), ())), preferred_element_type=F32,
                 )
 
         last = []
@@ -356,17 +377,18 @@
             total += land_c[i]
         out[...] = total
 
-    for cp in mom_out:
-        cp.start()
-    started = False
     steps = {"S0": s0, "S1": s1, "S2": s2, "S3": s3, "S4": s4, "T0": t0, "T1": t1, "T2": t2}
     for step in SEQ:
         i = int(step[-1])
         if step[0] == "S":
-            steps[step[:2]](2 * i)
-            steps[step[:2]](2 * i + 1)
+            steps[step[:2]](i)
         elif step[0] == "T":
-            steps[step[:2]](i)
+            steps[step[:2]](int(step[2]), i)
+        elif step[0] == "L":
+            load()
+        elif step[0] == "N":
+            for cp in mom_out:
+                cp.start()
         elif step[0] == "M":
             m0()
             for cp in trial_out:
@@ -419,7 +441,7 @@
             pltpu.VMEM((16, 8, 1024), F32),
             pltpu.VMEM((16, 256, 128), BF),
             pltpu.VMEM((16, 128, 128), BF),
-            pltpu.VMEM((64, 128), F32),
+            pltpu.VMEM((4, 64, 128), F32),
             pltpu.VMEM((256, 128), F32),
             pltpu.VMEM((128, 128), F32),
             pltpu.VMEM((16, 16, 128), F32),

time: 163 us -> 152 us (0.933)
  Pallas kernels: 159 us -> 147 us
    pallas_call x1, Pallas kernels: 159 us -> 147 us  [body(): pl.pallas_call(kernel, out_shape=jax.ShapeDtypeStruct((16, 128), F32), in...]
where the time goes in v2:
time: 152 us; the launch traced here: 150 us
  Pallas kernels  147 us (97%)
  local copies, waits for them, and re-layouts  2.34 us (2%)
    pallas_call x1, Pallas kernels, body(): pl.pallas_call(kernel, out_shape=jax.ShapeDtypeStruct((16, 128), F32), in...  147 us

profile of v2, /device:TPU:0, one launch (start us, length us, event | category | flops | bytes accessed | tf_op | source)
XLA Modules:
  0.0 150.0 jit_solution(15587645260176408474)
XLA Ops:
  0.0 0.8 reshape.14
  0.8 0.7 pad_maximum_fusion.trial
  1.4 146.9 %shard_map.73 = f32[16,128]{1,0:T(8,128)} custom-call(bf16[16,2048,128]{2,1,0:T(8,128)(2,1)} %w.1, bf16[32,16,128,128]{3,2,1,0:T(8,128)(2,1)} %bitcast.7, s32[2]{0:T(128)} %mom.1, s32[2]{0:T(128)} %count.1, s32[32]{0:T(128)} %rows.1, s32[32]{0:T(128)} %cols.1, bf16[16,128]{1,0:T(8,128)(2,1)} %pad_maximum_fusion.trial), custom_call_target="tpu_custom_call" | custom-call | tf_op jit(solution)/shard_map/pallas_call | solution.py:419
  148.4 0.8 reshape.15
  149.2 0.1 copy.8
  149.3 0.7 reshape.16
  (1 shorter events, 0.0 us)

commit v3 on v2

--- a/solution.py
+++ b/solution.py
@@ -10,6 +10,7 @@
 MESH = pl.DeviceIdType.MESH
 F32 = jnp.float32
 BF = jnp.bfloat16
+NCON = 8
 NU = 8
 NC = 4
 RC = 64
@@ -26,7 +27,7 @@
 )
 
 
-def kernel(w, dens, mom, count, rows, cols, trial, out, momv, moml, moms, *scratch):
+def kernel(w, dens, mom, count, rows, cols, trial_in, out, trial, tf, place, momv, moml, moms, *scratch):
     ag_b, ag_1, ag_2 = scratch[:NU], scratch[NU:NU + NC], scratch[NU + NC:NU + 2 * NC]
     (
         st_b, land_b, land_1, land_2,
@@ -97,6 +98,13 @@
                     local(dens.at[pair + 1], rv.at[b, :, :, lanes], psem.at[pair + 1]),
                 ))
 
+    tf[...] = jnp.zeros_like(tf)
+    vectors = trial_in[...].astype(F32)
+    for k in range(2):
+        for i in range(NCON):
+            tf[k * 8 + i:k * 8 + i + 1, 0:64] = vectors[k:k + 1, i * 64:i * 64 + 64]
+    low16 = lax.broadcasted_iota(jnp.int32, (16, 128), 1) < 64
+    trial[...] = jnp.where(low16, tf[...], pltpu.roll(tf[...], 64, 1)).astype(BF)
     lane8 = lax.broadcasted_iota(jnp.int32, (8, 128), 1)
     momv[...] = jnp.where(lane8 == 0, mom[0], mom[1])
     for g in range(3):
@@ -200,11 +208,11 @@
         me = mine[1 + p]
         for k in range(1, 8):
             d = (me + k) % 8
-            place = ag_b[u].at[(k - 1) // 2, pl.ds(2 * ((k - 1) % 2), 2)]
+            stage_at = ag_b[u].at[(k - 1) // 2, pl.ds(2 * ((k - 1) % 2), 2)]
             for s in range(2):
-                place[s] = ag[h][:, moms[1 + p, d, 0, s]].reshape(16, 16, 128)
+                stage_at[s] = ag[h][:, moms[1 + p, d, 0, s]].reshape(16, 16, 128)
             arrive_d[h] += go([copy_to(
-                place, land.at[me, h], asend.at[r, k - 1], arecv.at[r, k - 1], member(1 + p, d)
+                stage_at, land.at[me, h], asend.at[r, k - 1], arecv.at[r, k - 1], member(1 + p, d)
             )])
         for s in range(2):
             land[me, h, s] = ag[h][:, moms[1 + p, me, 0, s]].reshape(16, 16, 128)
@@ -293,6 +301,9 @@
             cp.wait()
         xr[kc] = trial[...]
         xc[kr] = trial[...]
+        src = lax.broadcasted_iota(jnp.int32, (128, 512), 0)
+        dst = lax.broadcasted_iota(jnp.int32, (128, 512), 1)
+        place[...] = ((src % 64) == (dst % 8) * 8 + dst // 64).astype(F32).astype(BF)
         low = lax.broadcasted_iota(jnp.int32, (8, 128), 1) < 64
         src = lax.broadcasted_iota(jnp.int32, (128, 1024), 0)
         dst = lax.broadcasted_iota(jnp.int32, (128, 1024), 1)
@@ -317,8 +328,8 @@
             p = 2 * pp
             listed = jnp.where(lane < 64, (p + 1) % 16, p % 16) < count[pp // 8]
             for pairs, band, table, size in ((rows, (lane // 8) % 8, pick_r, 256), (cols, lane % 8, pick_c, 128)):
-                place = jnp.where(lane < 64, pairs[p + 1], pairs[p])
-                key = jnp.where(listed, place * 8 + band, -1)
+                index = jnp.where(lane < 64, pairs[p + 1], pairs[p])
+                key = jnp.where(listed, index * 8 + band, -1)
                 at = lax.broadcasted_iota(jnp.int32, (size, 128), 0)
                 table[pp] = (at == key).astype(F32).astype(BF)
 
@@ -375,7 +386,16 @@
             total += land_r[i]
         for i in range(1, 8):
             total += land_c[i]
-        out[...] = total
+        parts = []
+        for _ in range(3):
+            parts.append(total.astype(BF))
+            total = total - parts[-1].astype(F32)
+        wide = jnp.dot(jnp.concatenate(parts, axis=0), place[...], preferred_element_type=F32)
+        wide = wide[0:16] + wide[16:32] + wide[32:48]
+        v = lax.broadcasted_iota(jnp.int32, (16, 512), 0) % 8
+        wide = jnp.where(v == (lax.broadcasted_iota(jnp.int32, (16, 512), 1) // 8) % 8, wide, 0.0)
+        for k in range(2):
+            out[k:k + 1] = jnp.sum(wide[k * 8:k * 8 + 8], axis=0, keepdims=True)
 
     steps = {"S0": s0, "S1": s1, "S2": s2, "S3": s3, "S4": s4, "T0": t0, "T1": t1, "T2": t2}
     for step in SEQ:
@@ -410,18 +430,19 @@
 
 
 def body(trial, screened, density, pair_rows, pair_cols, slot_momentum, slot_count):
-    half = trial.reshape(16, 64)
-    doubled = jnp.concatenate([half, half], axis=1)
     smem = pl.BlockSpec(memory_space=pltpu.SMEM)
     anywhere = pl.BlockSpec(memory_space=pl.ANY)
     vmem = pl.BlockSpec(memory_space=pltpu.VMEM)
     dma = pltpu.SemaphoreType.DMA
-    total = pl.pallas_call(
+    return pl.pallas_call(
         kernel,
-        out_shape=jax.ShapeDtypeStruct((16, 128), F32),
+        out_shape=jax.ShapeDtypeStruct((2, 512), F32),
         in_specs=[anywhere, anywhere, smem, smem, smem, smem, vmem],
         out_specs=vmem,
         scratch_shapes=[
+            pltpu.VMEM((16, 128), BF),
+            pltpu.VMEM((16, 128), F32),
+            pltpu.VMEM((128, 512), BF),
             pltpu.VMEM((8, 128), jnp.int32),
             pltpu.VMEM((3, 8, 8, 128), jnp.int32),
             pltpu.SMEM((3, 8, 8, 128), jnp.int32),
@@ -455,11 +476,8 @@
         ),
     )(
         screened, density.reshape(density.shape[0], 16, 128, 128),
-        slot_momentum, slot_count, pair_rows, pair_cols, doubled,
+        slot_momentum, slot_count, pair_rows, pair_cols, trial,
     )
-    total = total.reshape(2, 8, 2, 8, 8)
-    total = total[:, :, 0] + total[:, :, 1]
-    return total.transpose(0, 3, 1, 2).reshape(2, 512)
 
 
 def solution(mesh):

time: 152 us -> 150 us (0.987)
    reshape x3 -> x0, local copies, waits for them, and re-layouts: 2.25 us -> none  [the longest x1 0.79 us: body(): total = total.reshape(2, 8, 2, 8, 8)]
where the time goes in v3:
time: 150 us; the launch traced here: 148 us
  Pallas kernels  147 us (98%)
    pallas_call x1, Pallas kernels, body(): pl.pallas_call(kernel, out_shape=jax.ShapeDtypeStruct((2, 512), F32), in_...  147 us

profile of v3, /device:TPU:0, one launch (start us, length us, event | category | flops | bytes accessed | tf_op | source)
XLA Modules:
  0.0 148.4 jit_solution(16246168145243147786)
XLA Ops:
  0.0 147.1 %shard_map.73 = f32[2,512]{1,0:T(2,128)} custom-call(bf16[16,2048,128]{2,1,0:T(8,128)(2,1)} %w.1, bf16[32,16,128,128]{3,2,1,0:T(8,128)(2,1)} %bitcast.1, s32[2]{0:T(128)} %mom.1, s32[2]{0:T(128)} %count.1, s32[32]{0:T(128)} %rows.1, s32[32]{0:T(128)} %cols.1, bf16[2,512]{1,0:T(2,128)(2,1)} %trial_in.1), custom_call_target="tpu_custom_call" | custom-call | tf_op jit(solution)/shard_map/pallas_call | solution.py:437
  147.1 1.3 copy.9
